TPU v7x, 32 devices: a whole 2x2x4 slice. The times are simulated.
32 devices in a mesh: dom: 2 (over y), grp: 4 (over x, core), tp: 4 (over z).
Axes of the slice: x: 2, y: 2, z: 4, core: 2. Of those that a mesh axis runs over, the one named last changes fastest.
Arguments:
- acts: bfloat16 [4096, 8192], P(('dom', 'grp'), 'tp'), parts along dimension 0, may hold values from -6 to 6
- output_weight_matrix: bfloat16 [8192, 8192], P(None, 'tp'), may hold values from -0.0625 to 0.0625
- adapter_down_factors: bfloat16 [32, 8192, 64], P('grp', 'tp'), may hold values from -0.0625 to 0.0625
- adapter_up_factors: bfloat16 [32, 64, 8192], P('grp', None, 'tp'), may hold values from -0.75 to 0.75
- adapter_pairings: int32 [8, 4, 2], P('dom'), parts along dimension 0, may hold values from 0 to 7, as said below
- request_working_slot: int32 [4096], P(('dom', 'grp')), parts along dimension 0, may hold values from 0 to 7
Outputs:
- projected_out: bfloat16 [4096, 8192], P(('dom', 'grp'), 'tp'), parts along dimension 0
There are 2 independent parts, one for each index of `dom`. A program takes and returns all parts, laid end to end along the dimension named above; an argument that names none is the same for every part. Nothing has to cross between parts.
Inputs may be any that keep to these rules, and one draw needn't show every extreme that they name: The 2 entries adapter_pairings[s, d, :] of one pair differ.
All inputs are finite; a program needn't handle non-finite values.
Results may differ from a plain program's by a relative error of at most 0.0041.
Values may be sent and summed in bfloat16 or wider, within the bound.
A program may use at most 192 MiB of HBM per device.

v0:
```python
import jax
import jax.numpy as jnp
from jax import lax
from jax.sharding import PartitionSpec as P


def body(
    acts,
    output_weight_matrix,
    adapter_down_factors,
    adapter_up_factors,
    adapter_pairings,
    request_working_slot,
):
    groups = lax.axis_size("grp")
    group_index = lax.axis_index("grp")
    group_adapter_rows = adapter_down_factors.shape[0]
    down_all, up_all = (
        lax.all_gather(adapter_down_factors, "grp", axis=0, tiled=True),
        lax.all_gather(adapter_up_factors, "grp", axis=0, tiled=True),
    )
    column = jnp.take(adapter_pairings, group_index, axis=1)
    selected_adapter = (
        jnp.arange(groups, dtype=jnp.int32)[:, None] * group_adapter_rows + column
    ).reshape(-1)
    down_factor_rows = jnp.take(down_all, selected_adapter, axis=0)
    up_factor_rows = jnp.take(up_all, selected_adapter, axis=0)
    working = down_factor_rows.shape[0]
    rank_width = down_factor_rows.shape[2]
    batch_rows = acts.shape[0]
    columns = output_weight_matrix.shape[1]
    onehot = request_working_slot[:, None] == jnp.arange(working, dtype=jnp.int32)[None, :]
    scores = jnp.einsum("rd,wdk->rwk", acts, down_factor_rows, preferred_element_type=jnp.float32)
    partial_value = jnp.sum(jnp.where(onehot[:, :, None], scores, jnp.float32(0.0)), axis=1)
    rank_sum = lax.psum(partial_value, "tp")
    rank_bf = rank_sum.astype(jnp.bfloat16)
    spread = jnp.where(onehot[:, :, None], rank_bf[:, None, :], jnp.zeros((), jnp.bfloat16))
    spread = spread.reshape(batch_rows, working * rank_width)
    adapter_out = jnp.dot(
        spread,
        up_factor_rows.reshape(working * rank_width, columns),
        preferred_element_type=jnp.float32,
    )
    projected = jnp.dot(
        lax.all_gather(acts, "tp", axis=1, tiled=True),
        output_weight_matrix,
        preferred_element_type=jnp.float32,
    )
    return (projected + adapter_out).astype(jnp.bfloat16)


def solution(mesh):
    placed = (
        P(("dom", "grp"), "tp"),
        P(None, "tp"),
        P("grp", "tp", None),
        P("grp", None, "tp"),
        P("dom", None, None),
        P(("dom", "grp")),
    )
    return jax.shard_map(
        body, mesh=mesh, in_specs=placed, out_specs=P(("dom", "grp"), "tp"), check_vma=False
    )
```

profile of v0, /device:TPU:0, one launch (start us, length us, event | category | flops | bytes accessed | tf_op | source)
XLA Modules:
  0.0 316.5 jit_solution(2609953390174911784)
XLA Ops:
  6.5 0.0 all-gather.6.cloned.1.call-start
  6.5 0.7 all-gather.6.cloned.1.call-update
  7.3 0.0 copy-start
  7.3 0.0 copy-start.1
  7.3 0.0 all-gather.8.cloned.1.call-start
  7.3 0.7 all-gather.8.cloned.1.call-update
  8.0 0.0 all-gather.4.cloned.1.call-start
  8.1 0.7 all-gather.4.cloned.1.call-update
  8.8 0.0 copy-done
  8.8 0.1 dynamic-slice_select_fusion
  8.9 0.1 copy.13
  9.0 0.1 copy.14
  9.1 0.1 add.55
  9.1 0.1 add.53
  9.3 0.0 copy-done.1
  9.3 60.6 %all-gather.6.cloned.1.call-done = bf16[32,2048,64]{1,2,0:T(8,128)(2,1)} async-done(((bf16[8,2048,64]{1,2,0:T(8,128)(2,1)}), bf16[32,2048,64]{1,2,0:T(8,128)(2,1)}) %all-gather.6.cloned.1.call-update) | async-done | bytes 8388624 | tf_op jit(solution)/shard_map/all_gather | solution.py:19
  69.9 4.1 %gather_fusion = bf16[8,2048,64]{1,2,0:T(8,128)(2,1)S(1)} fusion(bf16[32,2048,64]{1,2,0:T(8,128)(2,1)} %all-gather.6.cloned.1.call-done, s32[1024]{0:T(1024)S(1)} %pad_clamp_fusion), kind=kCustom, calls=%fused_computation | custom fusion | bytes 4194336 | tf_op jit(solution)/shard_map/jit(_take)/gather | solution.py:26
  74.0 2.9 fusion.17
  76.9 52.9 %all-gather.8.cloned.1.call-done = bf16[32,64,2048]{2,1,0:T(8,128)(2,1)} async-done(((bf16[8,64,2048]{2,1,0:T(8,128)(2,1)}), bf16[32,64,2048]{2,1,0:T(8,128)(2,1)}) %all-gather.8.cloned.1.call-update) | async-done | bytes 8388624 | tf_op jit(solution)/shard_map/all_gather | solution.py:20
  129.8 4.1 %gather_fusion.1 = bf16[8,64,2048]{2,1,0:T(8,128)(2,1)S(1)} fusion(bf16[32,64,2048]{2,1,0:T(8,128)(2,1)} %all-gather.8.cloned.1.call-done, s32[1024]{0:T(1024)S(1)} %pad_clamp_fusion), kind=kCustom, calls=%fused_computation.1 | custom fusion | bytes 4194336 | tf_op jit(solution)/shard_map/jit(_take)/gather | solution.py:27
  133.9 28.7 %all-reduce.1 = bf16[512,64]{0,1:T(8,128)(2,1)S(1)} all-reduce(f32[512,64]{0,1:T(8,128)S(1)} %fusion.17), channel_id=1, replica_groups=mesh['dom'=2,'grp'=4,'tp'=4] {'tp'}, use_global_device_ids=true, to_apply=%region_1.2 | all-reduce | flops 32768 | bytes 196608 | tf_op jit(solution)/shard_map/psum | solution.py:35
  162.6 120.8 %all-gather.4.cloned.1.call-done = bf16[512,8192]{1,0:T(8,128)(2,1)} async-done(((bf16[512,2048]{1,0:T(8,128)(2,1)}), bf16[512,8192]{1,0:T(8,128)(2,1)}) %all-gather.4.cloned.1.call-update) | async-done | bytes 8388624 | tf_op jit(solution)/shard_map/all_gather | solution.py:45
  283.4 23.8 %fusion.32 = f32[512,2048]{1,0:T(8,128)S(1)} fusion(bf16[512,8192]{1,0:T(8,128)(2,1)} %all-gather.4.cloned.1.call-done, bf16[8192,2048]{1,0:T(8,128)(2,1)} %param.7), kind=kOutput, calls=%fused_computation.31 | convolution fusion | flops 17179869184 | bytes 46137344 | tf_op jit(solution)/shard_map/dot_general | solution.py:44
  307.2 2.8 fusion
  (6 shorter events, 0.0 us)
Async XLA Ops:
  6.5 63.4 %all-gather.6.cloned.1.call-start = ((), (), s32[]{:S(2)}) async-start(), calls=%async_computation.1 | async-start | bytes 10485760 | tf_op jit(solution)/shard_map/all_gather | solution.py:19
  7.3 1.5 copy-start
  7.3 2.0 copy-start.1
  7.3 122.5 %all-gather.8.cloned.1.call-start = ((), (), s32[]{:S(2)}) async-start(), calls=%async_computation.2 | async-start | bytes 10485760 | tf_op jit(solution)/shard_map/all_gather | solution.py:20
  8.0 275.4 %all-gather.4.cloned.1.call-start = ((), (), s32[]{:S(2)}) async-start(), calls=%async_computation | async-start | bytes 10485760 | tf_op jit(solution)/shard_map/all_gather | solution.py:45
Sparse Core Ops, SparseCore 0:
  8.9 60.9 all-gather.5
  71.5 58.2 all-gather.7
  131.4 151.9 all-gather.3
where the time goes:
time: 317 us
  waiting for transfers between devices  236 us (74%)
  matrix products  29.4 us (9%)
  blocking collectives  28.7 us (9%)
  between operations  13.2 us (4%)
  local copies, waits for them, and re-layouts  8.49 us (3%)
    all_gather x1, waiting for transfers between devices, body(): lax.all_gather(acts, 'tp', axis=1, tiled=True)  121 us
    all_gather x1, waiting for transfers between devices, body(): lax.all_gather(adapter_down_factors, 'grp', axis=0, tiled=True)  60.6 us
    all_gather x1, waiting for transfers between devices, body(): lax.all_gather(adapter_up_factors, 'grp', axis=0, tiled=True)  52.9 us
    psum x1, blocking collectives, body(): rank_sum = lax.psum(partial_value, 'tp')  28.7 us
    dot_general x1, matrix products, body(): jnp.dot(lax.all_gather(acts, 'tp', axis=1, tiled=True), output_weight_mat...  23.8 us
  transfers between devices with their start and end apart: 3, of which 3 were waited for; matrix products, arithmetic and copies ran while one was open for 4% of the time, Pallas kernels for 0%

commit v1 on v0

v1 whole, which is shorter than its diff:
```python
import functools

import jax
import jax.numpy as jnp
from jax import lax
from jax.experimental import pallas as pl
from jax.experimental.pallas import tpu as pltpu
from jax.sharding import PartitionSpec as P

MESH = pl.DeviceIdType.MESH


def divisor(size, most):
    return most if size % most == 0 else size


def kernel(
    tp, groups, chunks,
    acts, weight, down, up, pairings, slots, out,
    gathered, weights, acc, down_local, up_local, down_stage, up_stage, down_work, up_work,
    own_rank, low_in, low_out, high_in, high_out, staged,
    up_send, up_recv, dn_send, dn_recv, fac_send, fac_recv, rank_send, rank_recv,
    weight_sem, local_sem, out_sem,
):
    g, t = lax.axis_index("grp"), lax.axis_index("tp")
    batch, depth = acts.shape
    columns = weight.shape[1]
    rank = down.shape[2]
    rows = batch // chunks
    pair = pairings.shape[2]
    lanes = pair * rank
    half = batch // 2
    down_piece = down_local.shape[1]
    up_piece = up_local.shape[2]

    def row_block(c):
        return pl.ds(pl.multiple_of(c * rows, rows), rows)

    def peer(k):
        return lax.rem(g + k, groups)

    def weight_copy(j):
        return pltpu.make_async_copy(
            weight.at[pl.ds(pl.multiple_of(j * depth, depth), depth), :], weights.at[j], weight_sem.at[j]
        )

    own_copy = pltpu.make_async_copy(acts, gathered.at[t], local_sem.at[0])
    own_copy.start()

    barrier = pltpu.get_barrier_semaphore()

    @pl.when(t > 0)
    def _():
        pl.semaphore_signal(barrier, inc=1, device_id={"tp": t - 1}, device_id_type=MESH)

    @pl.when(t < tp - 1)
    def _():
        pl.semaphore_signal(barrier, inc=1, device_id={"tp": t + 1}, device_id_type=MESH)

    for k in range(1, groups):
        pl.semaphore_signal(barrier, inc=1, device_id={"grp": peer(k)}, device_id_type=MESH)
    pl.semaphore_wait(
        barrier, groups - 1 + jnp.where(t > 0, 1, 0) + jnp.where(t < tp - 1, 1, 0)
    )

    def own_send(c, to, send, recv):
        return pltpu.make_async_remote_copy(
            src_ref=acts.at[row_block(c), :], dst_ref=gathered.at[t, row_block(c), :],
            send_sem=send.at[0, c], recv_sem=recv.at[0, c],
            device_id={"tp": to}, device_id_type=MESH,
        )

    def passed(j, s, c, to, send, recv):
        return pltpu.make_async_remote_copy(
            src_ref=gathered.at[j, row_block(c), :], dst_ref=gathered.at[j, row_block(c), :],
            send_sem=send.at[s, c], recv_sem=recv.at[s, c],
            device_id={"tp": to}, device_id_type=MESH,
        )

    @pl.loop(0, chunks)
    def _(c):
        @pl.when(t > 0)
        def _():
            own_send(c, t - 1, dn_send, dn_recv).start()

        @pl.when(t < tp - 1)
        def _():
            own_send(c, t + 1, up_send, up_recv).start()

    def factor_send(which, k):
        stage, work = (down_stage, down_work) if which == 0 else (up_stage, up_work)
        return pltpu.make_async_remote_copy(
            src_ref=stage.at[peer(k)], dst_ref=work.at[g],
            send_sem=fac_send.at[which, k - 1], recv_sem=fac_recv.at[which, k - 1],
            device_id={"grp": peer(k)}, device_id_type=MESH,
        )

    def factor_own(which):
        stage, work = (down_stage, down_work) if which == 0 else (up_stage, up_work)
        return pltpu.make_async_copy(stage.at[g], work.at[g], local_sem.at[2])

    @pl.loop(0, depth // down_piece)
    def _(p):
        span = pl.ds(pl.multiple_of(p * down_piece, down_piece), down_piece)
        load = pltpu.make_async_copy(down.at[:, span, :], down_local, local_sem.at[1])
        load.start()
        load.wait()

        @pl.loop(0, groups)
        def _(d):
            down_stage[d, span, :] = jnp.concatenate(
                [down_local[pairings[g, d, k]] for k in range(pair)], axis=1
            )

    for k in range(1, groups):
        factor_send(0, k).start()
    factor_own(0).start()
    factor_own(0).wait()

    @pl.loop(0, columns // up_piece)
    def _(p):
        span = pl.ds(pl.multiple_of(p * up_piece, up_piece), up_piece)
        load = pltpu.make_async_copy(up.at[:, :, span], up_local, local_sem.at[1])
        load.start()
        load.wait()

        @pl.loop(0, groups)
        def _(d):
            for k in range(pair):
                up_stage[d, k * rank:(k + 1) * rank, span] = up_local[pairings[g, d, k]]

    for k in range(1, groups):
        factor_send(1, k).start()
    factor_own(1).start()
    factor_own(1).wait()

    @pl.loop(0, tp)
    def _(j):
        weight_copy(j).start()

    own_copy.wait()

    @pl.loop(0, tp)
    def _(j):
        weight_copy(j).wait()

    tile = divisor(columns, 512)

    def product(j, c, first):
        @pl.loop(0, columns // tile)
        def _(n):
            span = pl.ds(pl.multiple_of(n * tile, tile), tile)
            part = jnp.dot(
                gathered[j, row_block(c), :], weights[j, :, span], preferred_element_type=jnp.float32
            )
            if first:
                acc[row_block(c), span] = part
            else:
                acc[row_block(c), span] += part

    @pl.loop(0, chunks)
    def _(c):
        product(t, c, True)

    for k in range(1, groups):
        factor_send(0, k).wait_recv()
    lane = lax.broadcasted_iota(jnp.int32, (batch, lanes), 1)
    lane_pair = lane // rank

    def one_group(s, total):
        scores = jnp.dot(gathered[t], down_work[s], preferred_element_type=jnp.float32)
        return total + jnp.where(slots[...] == s * pair + lane_pair, scores, 0.0)

    chosen = lax.fori_loop(0, groups, one_group, jnp.zeros((batch, lanes), jnp.float32))
    folded = chosen + pltpu.roll(chosen, rank, 1)
    low_lane = lax.broadcasted_iota(jnp.int32, (half, lanes), 1) < rank
    own_rank[...] = jnp.where(low_lane, folded[:half], folded[half:])

    def rank_pass(way, to):
        source, target = (low_out, low_in) if way == 0 else (high_out, high_in)
        return pltpu.make_async_remote_copy(
            src_ref=source, dst_ref=target,
            send_sem=rank_send.at[way], recv_sem=rank_recv.at[way],
            device_id={"tp": to}, device_id_type=MESH,
        )

    @pl.when(t == 0)
    def _():
        low_out[...] = own_rank[...]
        rank_pass(0, t + 1).start()

    @pl.when(t == tp - 1)
    def _():
        high_out[...] = own_rank[...]
        rank_pass(1, t - 1).start()

    def rank_hop(s):
        @pl.when(t == s)
        def _():
            rank_pass(0, t).wait_recv()

            @pl.when(t < tp - 1)
            def _():
                low_out[...] = low_in[...] + own_rank[...]
                rank_pass(0, t + 1).start()

        @pl.when(t == tp - 1 - s)
        def _():
            rank_pass(1, t).wait_recv()

            @pl.when(t > 0)
            def _():
                high_out[...] = high_in[...] + own_rank[...]
                rank_pass(1, t - 1).start()

    def add_adapters():
        @pl.when(t > 0)
        def _():
            own_rank[...] += low_in[...]

        @pl.when(t < tp - 1)
        def _():
            own_rank[...] += high_in[...]

        packed = own_rank[...]
        turned = pltpu.roll(packed, rank, 1)
        sums = jnp.concatenate(
            [jnp.where(low_lane, packed, turned), jnp.where(low_lane, turned, packed)], axis=0
        )
        for k in range(1, groups):
            factor_send(1, k).wait_recv()

        @pl.loop(0, groups)
        def _(s):
            spread = jnp.where(slots[...] == s * pair + lane_pair, sums, 0.0).astype(jnp.bfloat16)

            @pl.loop(0, columns // tile)
            def _(n):
                span = pl.ds(pl.multiple_of(n * tile, tile), tile)
                acc[:, span] += jnp.dot(
                    spread, up_work[s, :, span], preferred_element_type=jnp.float32
                )

    def out_copy(c):
        return pltpu.make_async_copy(
            staged.at[row_block(c), :], out.at[row_block(c), :], out_sem.at[c]
        )

    @pl.loop(1, tp)
    def _(s):
        @pl.loop(0, chunks)
        def _(c):
            @pl.when(t >= s)
            def _():
                passed(t - s, s - 1, c, t, up_send, up_recv).wait_recv()

                @pl.when(t < tp - 1)
                def _():
                    passed(t - s, s, c, t + 1, up_send, up_recv).start()

            @pl.when(t + s < tp)
            def _():
                passed(t + s, s - 1, c, t, dn_send, dn_recv).wait_recv()

                @pl.when(t > 0)
                def _():
                    passed(t + s, s, c, t - 1, dn_send, dn_recv).start()

            @pl.when(c == 0)
            def _():
                rank_hop(s)

                @pl.when(s == tp - 1)
                def _():
                    add_adapters()

            @pl.when(t >= s)
            def _():
                product(t - s, c, False)

            @pl.when(t + s < tp)
            def _():
                product(t + s, c, False)

            @pl.when(s == tp - 1)
            def _():
                staged[row_block(c), :] = acc[row_block(c), :].astype(staged.dtype)
                out_copy(c).start()

    @pl.loop(0, tp)
    def _(s):
        @pl.loop(0, chunks)
        def _(c):
            @pl.when((t >= s) & (t < tp - 1))
            def _():
                passed(t, s, c, t, up_send, up_recv).wait_send()

            @pl.when((t + s < tp) & (t > 0))
            def _():
                passed(t, s, c, t, dn_send, dn_recv).wait_send()

    @pl.when(t < tp - 1)
    def _():
        rank_pass(0, t).wait_send()

    @pl.when(t > 0)
    def _():
        rank_pass(1, t).wait_send()

    for which in range(2):
        for k in range(1, groups):
            factor_send(which, k).wait_send()

    @pl.loop(0, chunks)
    def _(c):
        out_copy(c).wait()


def body(tp, groups, acts, weight, down, up, pairings, slots):
    batch, depth = acts.shape
    columns = weight.shape[1]
    held, _, rank = down.shape
    lanes = pairings.shape[2] * rank
    chunks = 4 if tp <= 8 else 1
    down_piece, up_piece = divisor(depth, 512), divisor(columns, 512)
    bf16, f32 = jnp.bfloat16, jnp.float32
    slot_lanes = jnp.broadcast_to(slots[:, None], (batch, lanes))
    anywhere = pl.BlockSpec(memory_space=pl.ANY)
    flops = 2 * batch * columns * depth * tp + 2 * batch * groups * lanes * (depth + columns)
    packed = pltpu.VMEM((batch // 2, lanes), f32)
    return pl.pallas_call(
        functools.partial(kernel, tp, groups, chunks),
        out_shape=jax.ShapeDtypeStruct((batch, columns), bf16),
        in_specs=[anywhere] * 4
        + [pl.BlockSpec(memory_space=pltpu.SMEM), pl.BlockSpec(memory_space=pltpu.VMEM)],
        out_specs=anywhere,
        scratch_shapes=[
            pltpu.VMEM((tp, batch, depth), bf16),
            pltpu.VMEM((tp, depth, columns), bf16),
            pltpu.VMEM((batch, columns), f32),
            pltpu.VMEM((held, down_piece, rank), bf16),
            pltpu.VMEM((held, rank, up_piece), bf16),
            pltpu.VMEM((groups, depth, lanes), bf16),
            pltpu.VMEM((groups, lanes, columns), bf16),
            pltpu.VMEM((groups, depth, lanes), bf16),
            pltpu.VMEM((groups, lanes, columns), bf16),
            packed, packed, packed, packed, packed,
            pltpu.VMEM((batch, columns), bf16),
            pltpu.SemaphoreType.DMA((tp, chunks)),
            pltpu.SemaphoreType.DMA((tp, chunks)),
            pltpu.SemaphoreType.DMA((tp, chunks)),
            pltpu.SemaphoreType.DMA((tp, chunks)),
            pltpu.SemaphoreType.DMA((2, groups)),
            pltpu.SemaphoreType.DMA((2, groups)),
            pltpu.SemaphoreType.DMA((2,)),
            pltpu.SemaphoreType.DMA((2,)),
            pltpu.SemaphoreType.DMA((tp,)),
            pltpu.SemaphoreType.DMA((3,)),
            pltpu.SemaphoreType.DMA((chunks,)),
        ],
        compiler_params=pltpu.CompilerParams(
            collective_id=0, has_side_effects=True, vmem_limit_bytes=62 << 20
        ),
        cost_estimate=pl.CostEstimate(
            flops=flops, bytes_accessed=2 * (weight.size + 3 * acts.size), transcendentals=0
        ),
    )(acts, weight, down, up, pairings, slot_lanes)


def solution(mesh):
    placed = (
        P(("dom", "grp"), "tp"),
        P(None, "tp"),
        P("grp", "tp", None),
        P("grp", None, "tp"),
        P("dom", None, None),
        P(("dom", "grp")),
    )
    return jax.shard_map(
        functools.partial(body, mesh.shape["tp"], mesh.shape["grp"]),
        mesh=mesh, in_specs=placed, out_specs=P(("dom", "grp"), "tp"), check_vma=False,
    )
```

time: 317 us -> 159 us (0.50)
  waiting for transfers between devices: 236 us -> 0 us
  Pallas kernels: 0 us -> 148 us
  matrix products: 29.4 us -> 0 us
  blocking collectives: 28.7 us -> 0 us
  between operations: 13.2 us -> 0.01 us
    all_gather x3 -> x0, waiting for transfers between devices: 234 us -> none  [the longest x1 121 us: body(): lax.all_gather(acts, 'tp', axis=1, tiled=True)]
    pallas_call x0 -> x1, Pallas kernels: none -> 148 us  [body(): pl.pallas_call(functools.partial(kernel, tp, groups, chunks), out_shape=j...]
    dot_general x3 -> x0, matrix products: 29.4 us -> none  [the longest x1 23.8 us: body(): jnp.dot(lax.all_gather(acts, 'tp', axis=1, tiled=True), output_weight_mat...]
    psum x1 -> x0, blocking collectives: 28.7 us -> none  [body(): rank_sum = lax.psum(partial_value, 'tp')]
    unnamed x4 -> x3, local copies, waits for them, and re-layouts: 0.01 us -> 9.32 us
    gather x2 -> x0, local copies, waits for them, and re-layouts: 8.12 us -> none  [the longest x1 4.06 us: body(): down_factor_rows = jnp.take(down_all, selected_adapter, axis=0)]
  transfers between devices with their start and end apart: 3 -> 0, of which waited for: 3 -> 0; matrix products, arithmetic and copies ran while one was open for 4% -> 0% of each run, Pallas kernels for 0% -> 0%
where the time goes in v1:
time: 159 us
  Pallas kernels  148 us (93%)
  local copies, waits for them, and re-layouts  10.8 us (7%)
    pallas_call x1, Pallas kernels, body(): pl.pallas_call(functools.partial(kernel, tp, groups, chunks), out_shape=j...  148 us
    unnamed x3, local copies, waits for them, and re-layouts  9.32 us

profile of v1, /device:TPU:0, one launch (start us, length us, event | category | flops | bytes accessed | tf_op | source)
XLA Modules:
  0.0 158.8 jit_solution(1813654263592782212)
XLA Ops:
  0.0 1.4 copy.8.pairings
  1.4 1.5 broadcast_in_dim.2.slots
  2.9 4.8 %copy.7.down = bf16[8,2048,64]{2,1,0:T(8,128)(2,1)} copy(bf16[8,2048,64]{1,2,0:T(8,128)(2,1)} %param.8) | data formatting | bytes 4194304 | tf_op args[2]
  7.7 147.9 %shard_map.64 = bf16[512,2048]{1,0:T(8,128)(2,1)} custom-call(bf16[512,2048]{1,0:T(8,128)(2,1)} %acts.1, bf16[8192,2048]{1,0:T(8,128)(2,1)} %weight.1, bf16[8,2048,64]{2,1,0:T(8,128)(2,1)} %copy.7.down, bf16[8,64,2048]{2,1,0:T(8,128)(2,1)} %up.1, s32[4,4,2]{2,1,0:T(4,128)} %copy.8.pairings, s32[512,128]{1,0:T(8,128)} %broadcast_in_dim.2.slots), custom_call_target="tpu_custom_call" | custom-call | flops 19327352832 | bytes 39845888 | tf_op jit(solution)/shard_map/pallas_call | solution.py:331
  155.6 3.2 %copy.10 = bf16[512,2048]{1,0:T(8,128)(2,1)} copy(bf16[512,2048]{1,0:T(8,128)(2,1)} %shard_map.64) | data formatting | bytes 4194304

commit v2 on v1

v2 whole, which is shorter than its diff:
```python
import functools

import jax
import jax.numpy as jnp
from jax import lax
from jax.experimental import pallas as pl
from jax.experimental.pallas import tpu as pltpu
from jax.sharding import PartitionSpec as P

MESH = pl.DeviceIdType.MESH


def divisor(size, most):
    return most if size % most == 0 else size


def kernel(
    tp, groups, chunks,
    acts, weight, down, up, pairings, slots, out,
    gathered, weights, acc, down_local, up_local, down_stage, up_stage, down_work, up_work,
    own_rank, low_in, low_out, high_in, high_out, sum_in, sum_out, slot_lanes, staged,
    up_send, up_recv, dn_send, dn_recv, fac_send, fac_recv, rank_send, rank_recv,
    weight_sem, own_sem, local_sem, out_sem,
):
    g, t = lax.axis_index("grp"), lax.axis_index("tp")
    batch, depth = acts.shape
    columns = weight.shape[1]
    rank = down.shape[1]
    part = depth // chunks
    pair = pairings.shape[1]
    lanes = pair * rank
    half = batch // 2

    def features(c):
        return pl.ds(pl.multiple_of(c * part, part), part)

    def peer(k):
        return lax.rem(g + k, groups)

    def weight_copy(j):
        return pltpu.make_async_copy(
            weight.at[pl.ds(pl.multiple_of(j * depth, depth), depth), :], weights.at[j], weight_sem.at[j]
        )

    def own_copy(c):
        return pltpu.make_async_copy(acts.at[:, features(c)], gathered.at[t * chunks + c], own_sem.at[c])

    barrier = pltpu.get_barrier_semaphore()

    @pl.when(t > 0)
    def _():
        pl.semaphore_signal(barrier, inc=1, device_id={"tp": t - 1}, device_id_type=MESH)

    @pl.when(t < tp - 1)
    def _():
        pl.semaphore_signal(barrier, inc=1, device_id={"tp": t + 1}, device_id_type=MESH)

    for k in range(1, groups):
        pl.semaphore_signal(barrier, inc=1, device_id={"grp": peer(k)}, device_id_type=MESH)
    pl.semaphore_wait(
        barrier, groups - 1 + jnp.where(t > 0, 1, 0) + jnp.where(t < tp - 1, 1, 0)
    )

    def own_send(c, to, send, recv):
        return pltpu.make_async_remote_copy(
            src_ref=acts.at[:, features(c)], dst_ref=gathered.at[t * chunks + c],
            send_sem=send.at[0, c], recv_sem=recv.at[0, c],
            device_id={"tp": to}, device_id_type=MESH,
        )

    def passed(j, s, c, to, send, recv):
        return pltpu.make_async_remote_copy(
            src_ref=gathered.at[j * chunks + c], dst_ref=gathered.at[j * chunks + c],
            send_sem=send.at[s, c], recv_sem=recv.at[s, c],
            device_id={"tp": to}, device_id_type=MESH,
        )

    @pl.loop(0, chunks)
    def _(c):
        @pl.when(t > 0)
        def _():
            own_send(c, t - 1, dn_send, dn_recv).start()

        @pl.when(t < tp - 1)
        def _():
            own_send(c, t + 1, up_send, up_recv).start()

    def factor_send(which, k):
        stage, work = (down_stage, down_work) if which == 0 else (up_stage, up_work)
        return pltpu.make_async_remote_copy(
            src_ref=stage.at[peer(k)], dst_ref=work.at[g],
            send_sem=fac_send.at[which, k - 1], recv_sem=fac_recv.at[which, k - 1],
            device_id={"grp": peer(k)}, device_id_type=MESH,
        )

    def factor_own(which):
        stage, work = (down_stage, down_work) if which == 0 else (up_stage, up_work)
        return pltpu.make_async_copy(stage.at[g], work.at[g], local_sem.at[2])

    @pl.loop(0, chunks)
    def _(c):
        own_copy(c).start()

    def pick(source, local, stage):
        piece = local.shape[2]

        @pl.loop(0, source.shape[2] // piece)
        def _(p):
            span = pl.ds(pl.multiple_of(p * piece, piece), piece)
            load = pltpu.make_async_copy(source.at[:, :, span], local, local_sem.at[1])
            load.start()
            load.wait()

            @pl.loop(0, groups)
            def _(d):
                for k in range(pair):
                    stage[d, k * rank:(k + 1) * rank, span] = local[pairings[g, k, d]]

    pick(down, down_local, down_stage)
    for k in range(1, groups):
        factor_send(0, k).start()
    factor_own(0).start()
    factor_own(0).wait()
    pick(up, up_local, up_stage)
    for k in range(1, groups):
        factor_send(1, k).start()
    factor_own(1).start()
    factor_own(1).wait()

    @pl.loop(0, tp)
    def _(j):
        weight_copy(j).start()

    @pl.loop(0, chunks)
    def _(c):
        own_copy(c).wait()

    @pl.loop(0, tp)
    def _(j):
        weight_copy(j).wait()

    tile = divisor(columns, 256)

    def product(j, c, first=False, last=False):
        @pl.loop(0, columns // tile)
        def _(n):
            span = pl.ds(pl.multiple_of(n * tile, tile), tile)
            value = jnp.dot(
                gathered[j * chunks + c], weights[j, features(c), span],
                preferred_element_type=jnp.float32,
            )
            if not first:
                value = acc[:, span] + value
            if last:
                staged[:, span] = value.astype(staged.dtype)
                out_copy(n).start()
            else:
                acc[:, span] = value

    def out_copy(n):
        span = pl.ds(pl.multiple_of(n * tile, tile), tile)
        return pltpu.make_async_copy(staged.at[:, span], out.at[:, span], out_sem.at[n])

    product(t, 0, True)

    @pl.loop(1, chunks)
    def _(c):
        product(t, c)

    for i in range(batch // 128):
        row = jnp.broadcast_to(slots[i:i + 1, :], (128, 128))
        slot_lanes[i * 128:(i + 1) * 128, :] = row.T

    for k in range(1, groups):
        factor_send(0, k).wait_recv()
    lane = lax.broadcasted_iota(jnp.int32, (batch, lanes), 1)
    lane_pair = lane // rank

    def one_group(s, total):
        def one_part(c, scores):
            return scores + lax.dot_general(
                gathered[t * chunks + c], down_work[s, :, features(c)], (((1,), (1,)), ((), ())),
                preferred_element_type=jnp.float32,
            )

        scores = lax.fori_loop(0, chunks, one_part, jnp.zeros((batch, lanes), jnp.float32))
        return total + jnp.where(slot_lanes[...] == s * pair + lane_pair, scores, 0.0)

    chosen = lax.fori_loop(0, groups, one_group, jnp.zeros((batch, lanes), jnp.float32))
    folded = chosen + pltpu.roll(chosen, rank, 1)
    low_lane = lax.broadcasted_iota(jnp.int32, (half, lanes), 1) < rank
    own_rank[...] = jnp.where(low_lane, folded[:half], folded[half:])

    def rank_pass(way, to):
        source, target = (low_out, low_in) if way == 0 else (high_out, high_in)
        return pltpu.make_async_remote_copy(
            src_ref=source, dst_ref=target,
            send_sem=rank_send.at[way], recv_sem=rank_recv.at[way],
            device_id={"tp": to}, device_id_type=MESH,
        )

    @pl.when(t == 0)
    def _():
        low_out[...] = own_rank[...]
        rank_pass(0, t + 1).start()

    @pl.when(t == tp - 1)
    def _():
        high_out[...] = own_rank[...]
        rank_pass(1, t - 1).start()

    def sum_pass(to):
        return pltpu.make_async_remote_copy(
            src_ref=sum_out, dst_ref=sum_in,
            send_sem=rank_send.at[2 + jnp.where(t > to, 1, 0)], recv_sem=rank_recv.at[2],
            device_id={"tp": to}, device_id_type=MESH,
        )

    inner = (t > 0) & (t < tp - 1)

    def rank_hop(s):
        @pl.when(inner & (t == s))
        def _():
            rank_pass(0, t).wait_recv()

            @pl.when(t < tp - 2)
            def _():
                low_out[...] = low_in[...] + own_rank[...]
                rank_pass(0, t + 1).start()

        @pl.when(inner & (t == tp - 1 - s))
        def _():
            rank_pass(1, t).wait_recv()

            @pl.when(t > 1)
            def _():
                high_out[...] = high_in[...] + own_rank[...]
                rank_pass(1, t - 1).start()

        @pl.when(inner & (s == tp - 2))
        def _():
            own_rank[...] += low_in[...] + high_in[...]
            sum_out[...] = own_rank[...].astype(sum_out.dtype)

            @pl.when(t == 1)
            def _():
                sum_pass(0).start()

            @pl.when(t == tp - 2)
            def _():
                sum_pass(tp - 1).start()

    def add_adapters():
        @pl.when(jnp.logical_not(inner))
        def _():
            sum_pass(t).wait_recv()
            own_rank[...] = sum_in[...].astype(jnp.float32)

        packed = own_rank[...]
        turned = pltpu.roll(packed, rank, 1)
        sums = jnp.concatenate(
            [jnp.where(low_lane, packed, turned), jnp.where(low_lane, turned, packed)], axis=0
        )
        for k in range(1, groups):
            factor_send(1, k).wait_recv()

        @pl.loop(0, groups)
        def _(s):
            spread = jnp.where(slot_lanes[...] == s * pair + lane_pair, sums, 0.0).astype(jnp.bfloat16)

            @pl.loop(0, columns // tile)
            def _(n):
                span = pl.ds(pl.multiple_of(n * tile, tile), tile)
                acc[:, span] += jnp.dot(
                    spread, up_work[s, :, span], preferred_element_type=jnp.float32
                )

    @pl.loop(1, tp)
    def _(s):
        @pl.loop(0, chunks)
        def _(c):
            @pl.when(t >= s)
            def _():
                passed(t - s, s - 1, c, t, up_send, up_recv).wait_recv()

                @pl.when(t < tp - 1)
                def _():
                    passed(t - s, s, c, t + 1, up_send, up_recv).start()

            @pl.when(t + s < tp)
            def _():
                passed(t + s, s - 1, c, t, dn_send, dn_recv).wait_recv()

                @pl.when(t > 0)
                def _():
                    passed(t + s, s, c, t - 1, dn_send, dn_recv).start()

            @pl.when(c == 0)
            def _():
                rank_hop(s)

                @pl.when(s == tp - 1)
                def _():
                    add_adapters()

            closing = (s == tp - 1) & (c == chunks - 1)

            @pl.when((t >= s) & jnp.logical_not(closing))
            def _():
                product(t - s, c)

            @pl.when((t + s < tp) & jnp.logical_not(closing))
            def _():
                product(t + s, c)

            @pl.when(closing & jnp.logical_not(inner))
            def _():
                product(tp - 1 - t, c, last=True)

            @pl.when(closing & inner)
            def _():
                @pl.loop(0, columns // tile)
                def _(n):
                    span = pl.ds(pl.multiple_of(n * tile, tile), tile)
                    staged[:, span] = acc[:, span].astype(staged.dtype)
                    out_copy(n).start()

    @pl.loop(0, tp)
    def _(s):
        @pl.loop(0, chunks)
        def _(c):
            @pl.when((t >= s) & (t < tp - 1))
            def _():
                passed(t, s, c, t, up_send, up_recv).wait_send()

            @pl.when((t + s < tp) & (t > 0))
            def _():
                passed(t, s, c, t, dn_send, dn_recv).wait_send()

    @pl.when(t < tp - 2)
    def _():
        rank_pass(0, t).wait_send()

    @pl.when(t > 1)
    def _():
        rank_pass(1, t).wait_send()

    @pl.when(t == 1)
    def _():
        sum_pass(0).wait_send()

    @pl.when(t == tp - 2)
    def _():
        sum_pass(tp - 1).wait_send()

    for which in range(2):
        for k in range(1, groups):
            factor_send(which, k).wait_send()

    @pl.loop(0, columns // tile)
    def _(n):
        out_copy(n).wait()


def body(tp, groups, acts, weight, down, up, pairings, slots):
    batch, depth = acts.shape
    columns = weight.shape[1]
    down = jnp.swapaxes(down, 1, 2)
    pairings = jnp.swapaxes(pairings, 1, 2)
    slots = slots.reshape(batch // 128, 128)
    held, rank, _ = down.shape
    lanes = pairings.shape[1] * rank
    part = divisor(depth, 256)
    chunks = depth // part
    tiles = columns // divisor(columns, 256)
    down_piece, up_piece = divisor(depth, 512), divisor(columns, 512)
    bf16, f32 = jnp.bfloat16, jnp.float32
    anywhere = pl.BlockSpec(memory_space=pl.ANY)
    flops = 2 * batch * columns * depth * tp + 2 * batch * groups * lanes * (depth + columns)
    packed = pltpu.VMEM((batch // 2, lanes), f32)
    return pl.pallas_call(
        functools.partial(kernel, tp, groups, chunks),
        out_shape=jax.ShapeDtypeStruct((batch, columns), bf16),
        in_specs=[anywhere] * 4
        + [pl.BlockSpec(memory_space=pltpu.SMEM), pl.BlockSpec(memory_space=pltpu.VMEM)],
        out_specs=anywhere,
        scratch_shapes=[
            pltpu.VMEM((tp * chunks, batch, part), bf16),
            pltpu.VMEM((tp, depth, columns), bf16),
            pltpu.VMEM((batch, columns), f32),
            pltpu.VMEM((held, rank, down_piece), bf16),
            pltpu.VMEM((held, rank, up_piece), bf16),
            pltpu.VMEM((groups, lanes, depth), bf16),
            pltpu.VMEM((groups, lanes, columns), bf16),
            pltpu.VMEM((groups, lanes, depth), bf16),
            pltpu.VMEM((groups, lanes, columns), bf16),
            packed, packed, packed, packed, packed,
            pltpu.VMEM((batch // 2, lanes), bf16),
            pltpu.VMEM((batch // 2, lanes), bf16),
            pltpu.VMEM((batch, lanes), jnp.int32),
            pltpu.VMEM((batch, columns), bf16),
            pltpu.SemaphoreType.DMA((tp, chunks)),
            pltpu.SemaphoreType.DMA((tp, chunks)),
            pltpu.SemaphoreType.DMA((tp, chunks)),
            pltpu.SemaphoreType.DMA((tp, chunks)),
            pltpu.SemaphoreType.DMA((2, groups)),
            pltpu.SemaphoreType.DMA((2, groups)),
            pltpu.SemaphoreType.DMA((4,)),
            pltpu.SemaphoreType.DMA((3,)),
            pltpu.SemaphoreType.DMA((tp,)),
            pltpu.SemaphoreType.DMA((chunks,)),
            pltpu.SemaphoreType.DMA((3,)),
            pltpu.SemaphoreType.DMA((tiles,)),
        ],
        compiler_params=pltpu.CompilerParams(
            collective_id=0, has_side_effects=True, vmem_limit_bytes=60 << 20
        ),
        cost_estimate=pl.CostEstimate(
            flops=flops, bytes_accessed=2 * (weight.size + 3 * acts.size), transcendentals=0
        ),
    )(acts, weight, down, up, pairings, slots)


def solution(mesh):
    placed = (
        P(("dom", "grp"), "tp"),
        P(None, "tp"),
        P("grp", "tp", None),
        P("grp", None, "tp"),
        P("dom", None, None),
        P(("dom", "grp")),
    )
    return jax.shard_map(
        functools.partial(body, mesh.shape["tp"], mesh.shape["grp"]),
        mesh=mesh, in_specs=placed, out_specs=P(("dom", "grp"), "tp"), check_vma=False,
    )
```

time: 159 us -> 153 us (0.962)
  local copies, waits for them, and re-layouts: 10.8 us -> 3.16 us
    unnamed x3 -> x1, local copies, waits for them, and re-layouts: 9.32 us -> 3.16 us
where the time goes in v2:
time: 153 us; the launch traced here: 152 us
  Pallas kernels  149 us (97%)
  local copies, waits for them, and re-layouts  3.16 us (2%)
    pallas_call x1, Pallas kernels, body(): pl.pallas_call(functools.partial(kernel, tp, groups, chunks), out_shape=j...  149 us
    unnamed x1, local copies, waits for them, and re-layouts  3.16 us

profile of v2, /device:TPU:0, one launch (start us, length us, event | category | flops | bytes accessed | tf_op | source)
XLA Modules:
  0.0 152.0 jit_solution(2786437999749493640)
XLA Ops:
  0.0 148.8 %shard_map.64 = bf16[512,2048]{1,0:T(8,128)(2,1)} custom-call(bf16[512,2048]{1,0:T(8,128)(2,1)} %acts.1, bf16[8192,2048]{1,0:T(8,128)(2,1)} %weight.1, bf16[8,64,2048]{2,1,0:T(8,128)(2,1)} %bitcast.3, bf16[8,64,2048]{2,1,0:T(8,128)(2,1)} %up.1, s32[4,2,4]{2,1,0:T(2,128)} %bitcast.4, s32[4,128]{1,0:T(4,128)} %bitcast.5), custom_call_target="tpu_custom_call" | custom-call | flops 19327352832 | bytes 39845888 | tf_op jit(solution)/shard_map/pallas_call | solution.py:381
  148.8 3.2 %copy.8 = bf16[512,2048]{1,0:T(8,128)(2,1)} copy(bf16[512,2048]{1,0:T(8,128)(2,1)} %shard_map.64) | data formatting | bytes 4194304

commit v3 on v2

--- a/solution.py
+++ b/solution.py
@@ -18,9 +18,9 @@
     tp, groups, chunks,
     acts, weight, down, up, pairings, slots, out,
     gathered, weights, acc, down_local, up_local, down_stage, up_stage, down_work, up_work,
-    own_rank, low_in, low_out, high_in, high_out, sum_in, sum_out, slot_lanes, staged,
+    own_rank, low_in, low_out, high_in, high_out, sum_in, sum_out, slot_lanes,
     up_send, up_recv, dn_send, dn_recv, fac_send, fac_recv, rank_send, rank_recv,
-    weight_sem, own_sem, local_sem, out_sem,
+    weight_sem, own_sem, local_sem,
 ):
     g, t = lax.axis_index("grp"), lax.axis_index("tp")
     batch, depth = acts.shape
@@ -152,14 +152,9 @@
             if not first:
                 value = acc[:, span] + value
             if last:
-                staged[:, span] = value.astype(staged.dtype)
-                out_copy(n).start()
+                out[:, span] = value.astype(out.dtype)
             else:
                 acc[:, span] = value
-
-    def out_copy(n):
-        span = pl.ds(pl.multiple_of(n * tile, tile), tile)
-        return pltpu.make_async_copy(staged.at[:, span], out.at[:, span], out_sem.at[n])
 
     product(t, 0, True)
 
@@ -322,8 +317,7 @@
                 @pl.loop(0, columns // tile)
                 def _(n):
                     span = pl.ds(pl.multiple_of(n * tile, tile), tile)
-                    staged[:, span] = acc[:, span].astype(staged.dtype)
-                    out_copy(n).start()
+                    out[:, span] = acc[:, span].astype(out.dtype)
 
     @pl.loop(0, tp)
     def _(s):
@@ -356,10 +350,6 @@
     for which in range(2):
         for k in range(1, groups):
             factor_send(which, k).wait_send()
-
-    @pl.loop(0, columns // tile)
-    def _(n):
-        out_copy(n).wait()
 
 
 def body(tp, groups, acts, weight, down, up, pairings, slots):
@@ -372,7 +362,6 @@
     lanes = pairings.shape[1] * rank
     part = divisor(depth, 256)
     chunks = depth // part
-    tiles = columns // divisor(columns, 256)
     down_piece, up_piece = divisor(depth, 512), divisor(columns, 512)
     bf16, f32 = jnp.bfloat16, jnp.float32
     anywhere = pl.BlockSpec(memory_space=pl.ANY)
@@ -380,10 +369,10 @@
     packed = pltpu.VMEM((batch // 2, lanes), f32)
     return pl.pallas_call(
         functools.partial(kernel, tp, groups, chunks),
-        out_shape=jax.ShapeDtypeStruct((batch, columns), bf16),
+        out_shape=pltpu.VMEM((batch, columns), bf16),
         in_specs=[anywhere] * 4
         + [pl.BlockSpec(memory_space=pltpu.SMEM), pl.BlockSpec(memory_space=pltpu.VMEM)],
-        out_specs=anywhere,
+        out_specs=pl.BlockSpec(memory_space=pltpu.VMEM),
         scratch_shapes=[
             pltpu.VMEM((tp * chunks, batch, part), bf16),
             pltpu.VMEM((tp, depth, columns), bf16),
@@ -398,7 +387,6 @@
             pltpu.VMEM((batch // 2, lanes), bf16),
             pltpu.VMEM((batch // 2, lanes), bf16),
             pltpu.VMEM((batch, lanes), jnp.int32),
-            pltpu.VMEM((batch, columns), bf16),
             pltpu.SemaphoreType.DMA((tp, chunks)),
             pltpu.SemaphoreType.DMA((tp, chunks)),
             pltpu.SemaphoreType.DMA((tp, chunks)),
@@ -410,10 +398,9 @@
             pltpu.SemaphoreType.DMA((tp,)),
             pltpu.SemaphoreType.DMA((chunks,)),
             pltpu.SemaphoreType.DMA((3,)),
-            pltpu.SemaphoreType.DMA((tiles,)),
         ],
         compiler_params=pltpu.CompilerParams(
-            collective_id=0, has_side_effects=True, vmem_limit_bytes=60 << 20
+            collective_id=0, has_side_effects=True, vmem_limit_bytes=57 << 20
         ),
         cost_estimate=pl.CostEstimate(
             flops=flops, bytes_accessed=2 * (weight.size + 3 * acts.size), transcendentals=0

time: 153 us -> 150 us (0.980)
  local copies, waits for them, and re-layouts: 3.16 us -> 1.32 us
    unnamed x1, local copies, waits for them, and re-layouts: 3.16 us -> 1.32 us
where the time goes in v3:
time: 150 us
  Pallas kernels  148 us (99%)
    pallas_call x1, Pallas kernels, body(): pl.pallas_call(functools.partial(kernel, tp, groups, chunks), out_shape=p...  148 us

profile of v3, /device:TPU:0, one launch (start us, length us, event | category | flops | bytes accessed | tf_op | source)
XLA Modules:
  0.0 149.7 jit_solution(2208505854718415242)
XLA Ops:
  0.0 148.4 %shard_map.64 = bf16[512,2048]{1,0:T(8,128)(2,1)S(1)} custom-call(bf16[512,2048]{1,0:T(8,128)(2,1)} %acts.1, bf16[8192,2048]{1,0:T(8,128)(2,1)} %weight.1, bf16[8,64,2048]{2,1,0:T(8,128)(2,1)} %bitcast.3, bf16[8,64,2048]{2,1,0:T(8,128)(2,1)} %up.1, s32[4,2,4]{2,1,0:T(2,128)} %bitcast.4, s32[4,128]{1,0:T(4,128)} %bitcast.5), custom_call_target="tpu_custom_call" | custom-call | flops 19327352832 | bytes 39845888 | tf_op jit(solution)/shard_map/pallas_call | solution.py:370
  148.4 1.3 copy.8

commit v4 on v3

--- a/solution.py
+++ b/solution.py
@@ -270,13 +270,21 @@
                     spread, up_work[s, :, span], preferred_element_type=jnp.float32
                 )
 
+    flight = min(2, chunks)
+
     @pl.loop(1, tp)
     def _(s):
         @pl.loop(0, chunks)
         def _(c):
+            paced = (s == tp - 2) & (c >= flight)
+
             @pl.when(t >= s)
             def _():
                 passed(t - s, s - 1, c, t, up_send, up_recv).wait_recv()
+
+                @pl.when((t < tp - 1) & paced)
+                def _():
+                    passed(t, s, c - flight, t, up_send, up_recv).wait_send()
 
                 @pl.when(t < tp - 1)
                 def _():
@@ -285,6 +293,10 @@
             @pl.when(t + s < tp)
             def _():
                 passed(t + s, s - 1, c, t, dn_send, dn_recv).wait_recv()
+
+                @pl.when((t > 0) & paced)
+                def _():
+                    passed(t, s, c - flight, t, dn_send, dn_recv).wait_send()
 
                 @pl.when(t > 0)
                 def _():
@@ -323,11 +335,13 @@
     def _(s):
         @pl.loop(0, chunks)
         def _(c):
-            @pl.when((t >= s) & (t < tp - 1))
+            left = (s != tp - 2) | (c >= chunks - flight)
+
+            @pl.when((t >= s) & (t < tp - 1) & left)
             def _():
                 passed(t, s, c, t, up_send, up_recv).wait_send()
 
-            @pl.when((t + s < tp) & (t > 0))
+            @pl.when((t + s < tp) & (t > 0) & left)
             def _():
                 passed(t, s, c, t, dn_send, dn_recv).wait_send()
 

time: 150 us -> 150 us (level)
  no operation moved by 1% of the time
where the time goes in v4:
time: 150 us
  Pallas kernels  148 us (99%)
    pallas_call x1, Pallas kernels, body(): pl.pallas_call(functools.partial(kernel, tp, groups, chunks), out_shape=p...  148 us

profile of v4, /device:TPU:0, one launch (start us, length us, event | category | flops | bytes accessed | tf_op | source)
XLA Modules:
  0.0 149.8 jit_solution(14272152602428569909)
XLA Ops:
  0.0 148.4 %shard_map.64 = bf16[512,2048]{1,0:T(8,128)(2,1)S(1)} custom-call(bf16[512,2048]{1,0:T(8,128)(2,1)} %acts.1, bf16[8192,2048]{1,0:T(8,128)(2,1)} %weight.1, bf16[8,64,2048]{2,1,0:T(8,128)(2,1)} %bitcast.3, bf16[8,64,2048]{2,1,0:T(8,128)(2,1)} %up.1, s32[4,2,4]{2,1,0:T(2,128)} %bitcast.4, s32[4,128]{1,0:T(4,128)} %bitcast.5), custom_call_target="tpu_custom_call" | custom-call | flops 19327352832 | bytes 39845888 | tf_op jit(solution)/shard_map/pallas_call | solution.py:384
  148.4 1.3 copy.8

commit v5 on v3

--- a/solution.py
+++ b/solution.py
@@ -139,7 +139,7 @@
     def _(j):
         weight_copy(j).wait()
 
-    tile = divisor(columns, 256)
+    tile = divisor(columns, 512)
 
     def product(j, c, first=False, last=False):
         @pl.loop(0, columns // tile)

time: 150 us -> 148 us (0.987)
  Pallas kernels: 148 us -> 146 us
    pallas_call x1, Pallas kernels: 148 us -> 146 us  [body(): pl.pallas_call(functools.partial(kernel, tp, groups, chunks), out_shape=p...]
where the time goes in v5:
time: 148 us
  Pallas kernels  146 us (99%)
    pallas_call x1, Pallas kernels, body(): pl.pallas_call(functools.partial(kernel, tp, groups, chunks), out_shape=p...  146 us

profile of v5, /device:TPU:0, one launch (start us, length us, event | category | flops | bytes accessed | tf_op | source)
XLA Modules:
  0.0 147.6 jit_solution(9260520504086756920)
XLA Ops:
  0.0 146.3 %shard_map.64 = bf16[512,2048]{1,0:T(8,128)(2,1)S(1)} custom-call(bf16[512,2048]{1,0:T(8,128)(2,1)} %acts.1, bf16[8192,2048]{1,0:T(8,128)(2,1)} %weight.1, bf16[8,64,2048]{2,1,0:T(8,128)(2,1)} %bitcast.3, bf16[8,64,2048]{2,1,0:T(8,128)(2,1)} %up.1, s32[4,2,4]{2,1,0:T(2,128)} %bitcast.4, s32[4,128]{1,0:T(4,128)} %bitcast.5), custom_call_target="tpu_custom_call" | custom-call | flops 19327352832 | bytes 39845888 | tf_op jit(solution)/shard_map/pallas_call | solution.py:370
  146.3 1.3 copy.8

commit v6 on v5

--- a/solution.py
+++ b/solution.py
@@ -139,7 +139,7 @@
     def _(j):
         weight_copy(j).wait()
 
-    tile = divisor(columns, 512)
+    tile = divisor(columns, 1024)
 
     def product(j, c, first=False, last=False):
         @pl.loop(0, columns // tile)

time: 148 us -> 147 us (level)
  no operation moved by 1% of the time
where the time goes in v6:
time: 147 us
  Pallas kernels  145 us (99%)
    pallas_call x1, Pallas kernels, body(): pl.pallas_call(functools.partial(kernel, tp, groups, chunks), out_shape=p...  145 us

profile of v6, /device:TPU:0, one launch (start us, length us, event | category | flops | bytes accessed | tf_op | source)
XLA Modules:
  0.0 146.8 jit_solution(10405474007279838429)
XLA Ops:
  0.0 145.4 %shard_map.64 = bf16[512,2048]{1,0:T(8,128)(2,1)S(1)} custom-call(bf16[512,2048]{1,0:T(8,128)(2,1)} %acts.1, bf16[8192,2048]{1,0:T(8,128)(2,1)} %weight.1, bf16[8,64,2048]{2,1,0:T(8,128)(2,1)} %bitcast.3, bf16[8,64,2048]{2,1,0:T(8,128)(2,1)} %up.1, s32[4,2,4]{2,1,0:T(2,128)} %bitcast.4, s32[4,128]{1,0:T(4,128)} %bitcast.5), custom_call_target="tpu_custom_call" | custom-call | flops 19327352832 | bytes 39845888 | tf_op jit(solution)/shard_map/pallas_call | solution.py:370
  145.5 1.3 copy.8
